TPU v7x, 32 devices: a whole 2x2x4 slice. The times are simulated.
32 devices in a mesh: group: 2 (over x), wide: 16 (over z, y, core).
Axes of the slice: x: 2, y: 2, z: 4, core: 2. Of those that a mesh axis runs over, the one named last changes fastest.
Arguments:
- hidden_in: bfloat16 [256, 8192], P(('group', 'wide')), parts along dimension 0, may hold values from -6 to 6
- norm_gain: float32 [8192], replicated, may hold values from 0.1 to 1.9
- q_tiles: bfloat16 [64, 32, 128, 128], P('wide'), may hold values from -0.09375 to 0.09375
- q_rows: int32 [64, 32], P('wide'), may hold values from 0 to 63, as said below
- kv_tiles: bfloat16 [64, 12, 128, 128], P('wide'), may hold values from -0.09375 to 0.09375
- kv_cols: int32 [64, 12], P('wide'), may hold values from 0 to 15, as said below
- kv_count: int32 [64], P('wide'), may hold values from 4 to 12
- o_tiles: bfloat16 [64, 32, 128, 128], P('wide'), may hold values from -0.09375 to 0.09375
- o_rows: int32 [64, 32], P('wide'), may hold values from 0 to 63, as said below
- k_cache: bfloat16 [256, 8, 256, 128], P(('group', 'wide')), parts along dimension 0, may hold values from -6 to 6
- v_cache: bfloat16 [256, 8, 256, 128], P(('group', 'wide')), parts along dimension 0, may hold values from -16 to 16
- lengths: int32 [256], P(('group', 'wide')), parts along dimension 0, may hold values from 1 to 255
Outputs:
- mixed: bfloat16 [256, 8192], P(('group', 'wide')), parts along dimension 0
- new_kv: bfloat16 [256, 2048], P(('group', 'wide')), parts along dimension 0
There are 2 independent parts, one for each index of `group`. A program takes and returns all parts, laid end to end along the dimension named above; an argument that names none is the same for every part. Nothing has to cross between parts.
Inputs may be any that keep to these rules, and one draw needn't show every extreme that they name: Each row of q_rows holds 32 different input row blocks. Each row of o_rows holds 32 different input row blocks. Each row of kv_cols holds different column blocks; slots at or after kv_count of the row are padding.
All inputs are finite; a program needn't handle non-finite values.
Results may differ from a plain program's by a relative error of at most 0.0084.
Values may be sent and summed in bfloat16 or wider, within the bound.
A program may use at most 128 MiB of HBM per device.

v0:
```python
import jax
import jax.numpy as jnp
from jax import lax
from jax.sharding import PartitionSpec as P


def sparse_columns(rows_x, tiles, index):
    side = tiles.shape[2]
    count = rows_x.shape[0]
    blocks_x = rows_x.reshape(count, -1, side)
    chosen = jnp.take(blocks_x, index, axis=1)
    product = jnp.einsum("rckd,ckde->rce", chosen, tiles, preferred_element_type=jnp.float32)
    return product.reshape(count, -1)


def placement_table(cols, count, slot_total, kv_blocks):
    slots = jnp.arange(slot_total, dtype=jnp.int32)
    valid_slot = slots[None, :] < count[:, None]
    targets = jnp.arange(kv_blocks, dtype=jnp.int32)
    return (cols[:, :, None] == targets[None, None, :]) & valid_slot[:, :, None]


def kv_terms(slice_x, tiles, cols, count, kv_blocks):
    side = tiles.shape[2]
    rows_count = slice_x.shape[0]
    blocks_x = slice_x.reshape(rows_count, -1, side)
    partial_value = jnp.einsum(
        "rbd,bkde->rbke", blocks_x, tiles, preferred_element_type=jnp.float32
    )
    placing = placement_table(cols, count, tiles.shape[1], kv_blocks).astype(jnp.float32)
    summed = jnp.einsum("rbke,bkc->rce", partial_value, placing, precision=lax.Precision.HIGHEST)
    return summed.reshape(rows_count, -1)


def rotate(values, position):
    half = values.shape[-1] // 2
    steps = jnp.arange(half, dtype=jnp.float32)
    inverse = jnp.exp(-jnp.log(10000.0) * 2.0 * steps / values.shape[-1])
    angle = position.reshape(position.shape + (1,) * (values.ndim - 1)) * inverse
    first = values[..., :half]
    second = values[..., half:]
    return jnp.concatenate(
        [
            first * jnp.cos(angle) - second * jnp.sin(angle),
            first * jnp.sin(angle) + second * jnp.cos(angle),
        ],
        axis=-1,
    )


def attend(query, kv, k_cache, v_cache, lengths):
    rows_count = query.shape[0]
    groups = k_cache.shape[1]
    head_dim = k_cache.shape[3]
    repeat = query.shape[1] // head_dim // groups
    position = lengths.astype(jnp.float32)
    q_heads = query.astype(jnp.float32).reshape(rows_count, groups, repeat, head_dim)
    q_rot = rotate(q_heads, position).astype(jnp.bfloat16)
    key_new = rotate(
        kv[:, : groups * head_dim].reshape(rows_count, groups, head_dim), position
    ).astype(jnp.bfloat16)
    value_new = (
        kv[:, groups * head_dim :].reshape(rows_count, groups, head_dim).astype(jnp.bfloat16)
    )
    new_kv = jnp.concatenate(
        [key_new.reshape(rows_count, -1), value_new.reshape(rows_count, -1)], axis=1
    )
    scale = head_dim ** (-0.5)
    scores = (
        jnp.einsum("bgrd,bgld->bgrl", q_rot, k_cache, preferred_element_type=jnp.float32) * scale
    )
    own = jnp.einsum("bgrd,bgd->bgr", q_rot, key_new, preferred_element_type=jnp.float32) * scale
    places = jnp.arange(k_cache.shape[2], dtype=jnp.int32)
    valid = (places[None, :] < lengths[:, None])[:, None, None, :]
    masked = jnp.where(valid, scores, -jnp.inf)
    top = jnp.maximum(jnp.max(masked, axis=-1), own)
    expo = jnp.exp(masked - top[..., None])
    own_expo = jnp.exp(own - top)
    total = jnp.sum(expo, axis=-1) + own_expo
    weights = (expo / total[..., None]).astype(jnp.bfloat16)
    own_weight = (own_expo / total).astype(jnp.bfloat16)
    context = jnp.einsum("bgrl,bgld->bgrd", weights, v_cache, preferred_element_type=jnp.float32)
    context = (
        context
        + own_weight.astype(jnp.float32)[..., None] * value_new.astype(jnp.float32)[:, :, None, :]
    )
    return (context.reshape(rows_count, -1).astype(jnp.bfloat16), new_kv)


def body(
    hidden_in,
    norm_gain,
    q_tiles,
    q_rows,
    kv_tiles,
    kv_cols,
    kv_count,
    o_tiles,
    o_rows,
    k_cache,
    v_cache,
    lengths,
):
    side = q_tiles.shape[2]
    kv_blocks = 2 * k_cache.shape[1] * k_cache.shape[3] // side
    wide_x = hidden_in.astype(jnp.float32)
    power = jnp.mean(wide_x * wide_x, axis=1, keepdims=True)
    normed = (wide_x * lax.rsqrt(power + 1e-05) * norm_gain).astype(jnp.bfloat16)
    projected = sparse_columns(
        lax.all_gather(normed, "wide", axis=0, tiled=True), q_tiles, q_rows
    ).astype(jnp.bfloat16)
    slices = lax.all_to_all(normed, "wide", split_axis=1, concat_axis=0, tiled=True)
    kv = lax.psum_scatter(
        kv_terms(slices, kv_tiles, kv_cols, kv_count, kv_blocks),
        "wide",
        scatter_dimension=0,
        tiled=True,
    )
    query = lax.all_to_all(projected, "wide", split_axis=0, concat_axis=1, tiled=True)
    context, new_kv = attend(query, kv, k_cache, v_cache, lengths)
    output_cols = sparse_columns(
        lax.all_gather(context, "wide", axis=0, tiled=True), o_tiles, o_rows
    ).astype(jnp.bfloat16)
    mixed = lax.all_to_all(output_cols, "wide", split_axis=0, concat_axis=1, tiled=True)
    return (mixed, new_kv)


def solution(mesh):
    return jax.shard_map(
        body,
        mesh=mesh,
        in_specs=(
            P(("group", "wide"), None),
            P(),
            P("wide", None, None, None),
            P("wide", None),
            P("wide", None, None, None),
            P("wide", None),
            P("wide"),
            P("wide", None, None, None),
            P("wide", None),
            P(("group", "wide"), None, None, None),
            P(("group", "wide"), None, None, None),
            P(("group", "wide")),
        ),
        out_specs=(P(("group", "wide"), None), P(("group", "wide"), None)),
        check_vma=False,
    )
```

profile of v0, /device:TPU:0, one launch (start us, length us, event | category | flops | bytes accessed | tf_op | source)
XLA Modules:
  0.0 242.0 jit_solution(9554005128237909970)
XLA Ops:
  7.2 1.2 fusion.34
  8.4 1.7 fusion.36
  10.1 7.4 %all-to-all-start.1 = ((bf16[8,16,512]{2,0,1:T(8,128)(2,1)}), bf16[8,16,512]{2,0,1:T(8,128)(2,1)S(1)}, u32[]{:S(2)}, u32[]{:S(2)}) async-start(bf16[8,16,512]{2,0,1:T(8,128)(2,1)} %bitcast.8), calls=%async_computation.1 | async-start | bytes 262144 | tf_op jit(solution)/shard_map/all_to_all | solution.py:112
  17.5 0.7 iota_compare_fusion.2
  18.2 7.2 %all-to-all-done.1 = bf16[8,16,512]{2,0,1:T(8,128)(2,1)S(1)} async-done(((bf16[8,16,512]{2,0,1:T(8,128)(2,1)}), bf16[8,16,512]{2,0,1:T(8,128)(2,1)S(1)}, u32[]{:S(2)}, u32[]{:S(2)}) %all-to-all-start.1) | async-done | bytes 131104 | tf_op jit(solution)/shard_map/all_to_all | solution.py:112
  25.4 0.6 convolution_bitcast_fusion
  26.0 3.8 %fusion.4 = f32[16,128,128,1]{2,0,3,1:T(8,128)S(1)} fusion(f32[128,4,12,128]{3,0,2,1:T(8,128)S(1)} %convolution_bitcast_fusion, s32[4,12]{1,0:T(4,128)S(1)} %copy-done.3, pred[4,12]{1,0:T(4,128)(4,1)S(1)} %iota_compare_fusion.2), kind=kOutput, calls=%fused_computation.6 | convolution fusion | flops 150996480 | bytes 4194544 | tf_op jit(solution)/shard_map/rbke,bkc->rce/dot_general | solution.py:31
  29.9 1.3 copy.74
  31.2 0.0 all-gather.3.cloned.1.call-start
  31.3 0.7 all-gather.3.cloned.1.call-update
  32.0 0.1 reshape.258
  32.1 0.1 iota_compare_fusion.1
  32.2 0.1 multiply_cosine_fusion
  32.3 54.1 %reduce-scatter.2.cloned.1.call-done = f32[8,2048]{1,0:T(8,128)} async-done(((f32[128,2048]{1,0:T(8,128)}), f32[8,2048]{1,0:T(8,128)}) %reduce-scatter.2.cloned.1.call-update) | async-done | bytes 65552 | tf_op jit(solution)/shard_map/reduce_scatter | solution.py:113
  86.4 0.8 bitcast_convert_fusion
  87.2 0.8 slice_bitcast_fusion
  88.0 41.9 %all-gather.3.cloned.1.call-done = bf16[128,8192]{1,0:T(8,128)(2,1)} async-done(((bf16[8,8192]{1,0:T(8,128)(2,1)}), bf16[128,8192]{1,0:T(8,128)(2,1)}) %all-gather.3.cloned.1.call-update) | async-done | bytes 2097168 | tf_op jit(solution)/shard_map/all_gather | solution.py:110
  129.8 4.1 %copy.46 = bf16[128,8192]{0,1:T(8,128)(2,1)} copy(bf16[128,8192]{1,0:T(8,128)(2,1)} %all-gather.3.cloned.1.call-done) | data formatting | bytes 4194304 | tf_op jit(solution)/shard_map/all_gather | solution.py:110
  133.9 4.1 %copy.47 = bf16[128,64,128]{2,0,1:T(8,128)(2,1)} copy(bf16[128,64,128]{0,2,1:T(8,128)(2,1)} %bitcast.83) | data formatting | bytes 4194304 | tf_op jit(solution)/shard_map/reshape | solution.py:10
  138.0 4.6 %gather_fusion = bf16[128,128,128]{2,1,0:T(8,128)(2,1)} fusion(bf16[128,64,128]{2,0,1:T(8,128)(2,1)} %copy.47, s32[1024]{0:T(1024)S(1)} %pad_clamp_fusion.1), kind=kCustom, calls=%fused_computation.clone | custom fusion | bytes 8389120 | tf_op jit(solution)/shard_map/jit(_take)/gather | solution.py:11
  142.6 4.8 %fusion.26 = bf16[128,4,128]{2,0,1:T(8,128)(2,1)S(1)} fusion(bf16[4,32,128,128]{3,2,1,0:T(8,128)(2,1)} %param.16, bf16[4,32,128,128]{3,2,1,0:T(8,128)(2,1)} %bitcast.85, pred[4,32]{1,0:T(4,128)(4,1)S(1)} %compare_and_fusion.1), kind=kOutput, calls=%fused_computation.23 | convolution fusion | flops 539033600 | bytes 8519808 | tf_op jit(solution)/shard_map/rckd,ckde->rce/dot_general | solution.py:12
  147.4 0.1 copy.48
  147.5 0.7 convert_element_type.86
  148.2 3.5 %all-to-all-start = ((bf16[16,8,512]{2,1,0:T(8,128)(2,1)}), bf16[16,8,512]{2,1,0:T(8,128)(2,1)S(1)}, u32[]{:S(2)}, u32[]{:S(2)}) async-start(bf16[16,8,512]{2,1,0:T(8,128)(2,1)} %convert_element_type.86), calls=%async_computation | async-start | bytes 262144 | tf_op jit(solution)/shard_map/all_to_all | solution.py:119
  151.7 0.2 all-gather.5.cloned.1.call-start
  151.9 0.1 multiply_subtract_fusion
  152.0 0.1 fusion.55
  152.1 7.5 %all-to-all-done = bf16[16,8,512]{2,1,0:T(8,128)(2,1)S(1)} async-done(((bf16[16,8,512]{2,1,0:T(8,128)(2,1)}), bf16[16,8,512]{2,1,0:T(8,128)(2,1)S(1)}, u32[]{:S(2)}, u32[]{:S(2)}) %all-to-all-start) | async-done | bytes 131104 | tf_op jit(solution)/shard_map/all_to_all | solution.py:119
  159.6 0.2 copy.49
  159.8 0.1 subtract_convert_fusion
  160.0 0.3 fusion.40
  160.3 3.7 %fusion.53 = (f32[8,8,8]{2,1,0:T(8,128)S(1)}, f32[8,8,8,256]{3,2,1,0:T(8,128)S(1)}) fusion(bf16[8,8,256,128]{3,2,1,0:T(8,128)(2,1)} %param.23, bf16[8,8,8,64]{3,2,1,0:T(8,128)(2,1)S(1)} %get-tuple-element.6, bf16[8,8,8,64]{3,2,1,0:T(8,128)(2,1)S(1)} %get-tuple-element.5, pred[8,256]{1,0:T(8,128)(4,1)S(1)} %iota_compare_fusion.1), kind=kOutput, calls=%fused_computation.78 | convolution fusion | flops 34209280 | bytes 4853760 | tf_op jit(solution)/shard_map/bgrd,bgld->bgrl/dot_general | solution.py:70
  164.0 0.3 fusion.33
  164.3 0.7 fusion.32
  165.1 0.8 copy.75
  165.9 0.1 reshape.262
  166.0 39.1 %all-gather.5.cloned.1.call-done = bf16[128,8192]{1,0:T(8,128)(2,1)} async-done(((bf16[8,8192]{1,0:T(8,128)(2,1)}), bf16[128,8192]{1,0:T(8,128)(2,1)}) %all-gather.5.cloned.1.call-update) | async-done | bytes 2097168 | tf_op jit(solution)/shard_map/all_gather | solution.py:122
  205.0 4.1 %copy.53 = bf16[128,8192]{0,1:T(8,128)(2,1)} copy(bf16[128,8192]{1,0:T(8,128)(2,1)} %all-gather.5.cloned.1.call-done) | data formatting | bytes 4194304 | tf_op jit(solution)/shard_map/all_gather | solution.py:122
  209.1 4.1 %copy.54 = bf16[128,64,128]{2,0,1:T(8,128)(2,1)} copy(bf16[128,64,128]{0,2,1:T(8,128)(2,1)} %bitcast.84) | data formatting | bytes 4194304 | tf_op jit(solution)/shard_map/reshape | solution.py:10
  213.2 4.6 %gather_fusion.1 = bf16[128,128,128]{2,1,0:T(8,128)(2,1)} fusion(bf16[128,64,128]{2,0,1:T(8,128)(2,1)} %copy.54, s32[1024]{0:T(1024)S(1)} %pad_clamp_fusion), kind=kCustom, calls=%fused_computation.1.clone | custom fusion | bytes 8389120 | tf_op jit(solution)/shard_map/jit(_take)/gather | solution.py:11
  217.8 4.8 %fusion.29 = bf16[128,4,128]{2,0,1:T(8,128)(2,1)S(1)} fusion(bf16[4,32,128,128]{3,2,1,0:T(8,128)(2,1)} %param.21, bf16[4,32,128,128]{3,2,1,0:T(8,128)(2,1)} %bitcast.86, pred[4,32]{1,0:T(4,128)(4,1)S(1)} %compare_and_fusion), kind=kOutput, calls=%fused_computation.24 | convolution fusion | flops 539033600 | bytes 8519808 | tf_op jit(solution)/shard_map/rckd,ckde->rce/dot_general | solution.py:12
  222.6 0.1 copy.55
  222.7 0.7 convert_element_type.102
  223.4 3.5 %all-to-all-start.2 = ((bf16[16,8,512]{2,1,0:T(8,128)(2,1)}), bf16[16,8,512]{2,1,0:T(8,128)(2,1)S(1)}, u32[]{:S(2)}, u32[]{:S(2)}) async-start(bf16[16,8,512]{2,1,0:T(8,128)(2,1)} %convert_element_type.102), calls=%async_computation.3 | async-start | bytes 262144 | tf_op jit(solution)/shard_map/all_to_all | solution.py:124
  226.9 0.1 fusion.54
  227.0 0.6 pad_maximum_fusion.1
  227.6 7.2 %all-to-all-done.2 = bf16[16,8,512]{2,1,0:T(8,128)(2,1)S(1)} async-done(((bf16[16,8,512]{2,1,0:T(8,128)(2,1)}), bf16[16,8,512]{2,1,0:T(8,128)(2,1)S(1)}, u32[]{:S(2)}, u32[]{:S(2)}) %all-to-all-start.2) | async-done | bytes 131104 | tf_op jit(solution)/shard_map/all_to_all | solution.py:124
  234.8 0.7 copy.77
  (30 shorter events, 0.3 us)
Async XLA Ops:
  7.2 18.3 %copy-start = (bf16[4,12,128,128]{3,2,1,0:T(8,128)(2,1)S(1)}, bf16[4,12,128,128]{3,2,1,0:T(8,128)(2,1)}, u32[]{:S(2)}) copy-start(bf16[4,12,128,128]{3,2,1,0:T(8,128)(2,1)} %param.18) | copy-start | bytes 4718596
  7.2 18.8 %copy-start.3 = (s32[4,12]{1,0:T(4,128)S(1)}, s32[4,12]{1,0:T(4,128)}, u32[]{:S(2)}) copy-start(s32[4,12]{1,0:T(4,128)} %param.19) | copy-start | bytes 580
  10.1 15.3 %all-to-all-start.1 = ((bf16[8,16,512]{2,0,1:T(8,128)(2,1)}), bf16[8,16,512]{2,0,1:T(8,128)(2,1)S(1)}, u32[]{:S(2)}, u32[]{:S(2)}) async-start(bf16[8,16,512]{2,0,1:T(8,128)(2,1)} %bitcast.8), calls=%async_computation.1 | async-start | bytes 262144 | tf_op jit(solution)/shard_map/all_to_all | solution.py:112
  17.5 69.0 %reduce-scatter.2.cloned.1.call-start = ((), (), s32[]{:S(2)}) async-start(), calls=%async_computation.5 | async-start | bytes 1114112 | tf_op jit(solution)/shard_map/reduce_scatter | solution.py:113
  26.0 6.0 %copy-start.4 = (s32[8]{0:T(128)S(1)}, s32[8]{0:T(128)}, u32[]{:S(2)}) copy-start(s32[8]{0:T(128)} %param.25) | copy-start | bytes 100
  26.0 6.0 %copy-start.1 = (s32[4,32]{1,0:T(4,128)S(1)}, s32[4,32]{1,0:T(4,128)}, u32[]{:S(2)}) copy-start(s32[4,32]{1,0:T(4,128)} %param.17) | copy-start | bytes 1540
  31.2 98.6 %all-gather.3.cloned.1.call-start = ((), (), s32[]{:S(2)}) async-start(), calls=%async_computation.4 | async-start | bytes 2228224 | tf_op jit(solution)/shard_map/all_gather | solution.py:110
  148.2 11.4 %all-to-all-start = ((bf16[16,8,512]{2,1,0:T(8,128)(2,1)}), bf16[16,8,512]{2,1,0:T(8,128)(2,1)S(1)}, u32[]{:S(2)}, u32[]{:S(2)}) async-start(bf16[16,8,512]{2,1,0:T(8,128)(2,1)} %convert_element_type.86), calls=%async_computation | async-start | bytes 262144 | tf_op jit(solution)/shard_map/all_to_all | solution.py:119
  151.7 53.3 %all-gather.5.cloned.1.call-start = ((), (), s32[]{:S(2)}) async-start(), calls=%async_computation.6 | async-start | bytes 2228224 | tf_op jit(solution)/shard_map/all_gather | solution.py:122
  159.8 4.5 %copy-start.5 = (bf16[8,8,256,128]{3,2,1,0:T(8,128)(2,1)S(1)}, bf16[8,8,256,128]{3,2,1,0:T(8,128)(2,1)}, u32[]{:S(2)}) copy-start(bf16[8,8,256,128]{3,2,1,0:T(8,128)(2,1)} %param.24) | copy-start | bytes 12582916
  164.0 1.9 copy-start.2
  223.4 11.4 %all-to-all-start.2 = ((bf16[16,8,512]{2,1,0:T(8,128)(2,1)}), bf16[16,8,512]{2,1,0:T(8,128)(2,1)S(1)}, u32[]{:S(2)}, u32[]{:S(2)}) async-start(bf16[16,8,512]{2,1,0:T(8,128)(2,1)} %convert_element_type.102), calls=%async_computation.3 | async-start | bytes 262144 | tf_op jit(solution)/shard_map/all_to_all | solution.py:124
Sparse Core Ops, SparseCore 0:
  31.3 55.0 reduce-scatter.1
  89.4 40.3 all-gather.2
  166.0 39.0 all-gather.4
where the time goes:
time: 243 us; the launch traced here: 242 us
  waiting for transfers between devices  158 us (65%)
  local copies, waits for them, and re-layouts  31.1 us (13%)
  matrix products  18.7 us (8%)
  starting transfers between devices  14.7 us (6%)
  between operations  14 us (6%)
  other arithmetic  5.94 us (2%)
    reduce_scatter x1, waiting for transfers between devices, body(): lax.psum_scatter(kv_terms(slices, kv_tiles, kv_cols, kv_count, kv_blocks)...  54.1 us
    all_gather x1, waiting for transfers between devices, body(): lax.all_gather(normed, 'wide', axis=0, tiled=True)  41.9 us
    all_gather x1, waiting for transfers between devices, body(): lax.all_gather(context, 'wide', axis=0, tiled=True)  39.1 us
    dot_general x2, matrix products, sparse_columns(): jnp.einsum('rckd,ckde->rce', chosen, tiles, preferred_element_type=jnp.fl...  9.54 us
    gather x2, local copies, waits for them, and re-layouts, sparse_columns(): chosen = jnp.take(blocks_x, index, axis=1)  9.26 us
    reshape x2, local copies, waits for them, and re-layouts, sparse_columns(): blocks_x = rows_x.reshape(count, -1, side)  8.14 us
    all_to_all x1, waiting for transfers between devices, body(): lax.all_to_all(projected, 'wide', split_axis=0, concat_axis=1, tiled=True)  7.5 us
    all_to_all x1, starting transfers between devices, body(): lax.all_to_all(normed, 'wide', split_axis=1, concat_axis=0, tiled=True)  7.39 us
  transfers between devices with their start and end apart: 6, of which 6 were waited for; matrix products, arithmetic and copies ran while one was open for 1% of the time, Pallas kernels for 0%

commit v1 on v0

v1 whole, which is shorter than its diff:
```python
import functools

import jax
import jax.numpy as jnp
from jax import lax
from jax.experimental import pallas as pl
from jax.experimental.pallas import tpu as pltpu
from jax.sharding import PartitionSpec as P

MESH = pl.DeviceIdType.MESH
F32 = jnp.float32
BF16 = jnp.bfloat16
SUB = 8


def pack(blocks, paired):
    if paired:
        return [
            jnp.concatenate([blocks[2 * i], blocks[2 * i + 1]], axis=1).astype(BF16)
            for i in range(len(blocks) // 2)
        ]
    return [b.astype(BF16).astype(F32) for b in blocks]


def kernel(
    wide, ychips,
    lengths, q_rows, kv_cols, kv_count, o_rows, hidden, gain,
    q_hbm, kv_hbm, o_hbm, k_hbm, v_hbm,
    mixed, new_kv,
    qt, kt, ot, kc, vc,
    own1, sib1, own2, sib2, g1, g2, dense,
    kp, kr, ks, kf, qs, qr, os_, or_, qrot, knew, vnew,
    load_sem, x_send, x_recv, z_send, y_send, c_send, g_recv,
    k_send, k_recv, a_send, a_recv,
):
    chips = wide // 2
    zchips = chips // ychips
    me = lax.axis_index("wide")
    core = lax.rem(me, 2)
    chip = me // 2
    y = lax.rem(chip, ychips)
    z = chip // ychips
    sib = me + 1 - 2 * core
    nb, keep = q_rows.shape
    blocks = gain.shape[0]
    half = blocks // 2
    slots = kv_cols.shape[1]
    seqs, groups, cache = kc.shape[0], kc.shape[1], kc.shape[2]
    kvb = 2 * groups
    repeat = blocks // groups
    rows = wide * seqs
    paired = nb % 2 == 0

    def rcopy(src, dst, ss, rs, peer):
        return pltpu.make_async_remote_copy(
            src_ref=src, dst_ref=dst, send_sem=ss, recv_sem=rs,
            device_id={"wide": peer}, device_id_type=MESH)

    def dev(zz, yy, cc):
        return (zz * ychips + yy) * 2 + cc

    barrier = pltpu.get_barrier_semaphore()

    @pl.loop(1, wide)
    def _(s):
        pl.semaphore_signal(barrier, inc=1, device_id={"wide": lax.rem(me + s, wide)}, device_id_type=MESH)

    loads = [pltpu.make_async_copy(a, b, load_sem.at[i])
             for i, (a, b) in enumerate(((kv_hbm, kt), (q_hbm, qt), (k_hbm, kc), (v_hbm, vc), (o_hbm, ot)))]
    for cp in loads:
        cp.start()

    x = hidden[...].astype(F32)
    r = lax.rsqrt(jnp.mean(x * x, axis=1, keepdims=True) + 1e-05)
    for j in range(blocks):
        n = x[:, 128 * j:128 * (j + 1)] * r * gain[j:j + 1, :]
        own1[SUB * j:SUB * (j + 1), :] = n.astype(BF16).astype(F32)

    pl.semaphore_wait(barrier, wide - 1)

    def exchange(phase, own, got, g):
        hr = half * SUB
        cp = rcopy(own.at[pl.ds(pl.multiple_of(hr * (1 - core), hr), hr)], got,
                   x_send.at[phase], x_recv.at[phase], sib)
        cp.start()
        cp.wait_recv()
        a = own[pl.ds(pl.multiple_of(hr * core, hr), hr), :].reshape(half, SUB, 128)
        b = got[...].reshape(half, SUB, 128)
        first = jnp.where(core == 0, a, b)
        second = jnp.where(core == 0, b, a)
        g[chip, pl.ds(half * core, half)] = jnp.concatenate([first, second], axis=1).astype(BF16)
        return cp

    def gather(phase, g):
        def unit(zz, yy, cc):
            return g.at[zz * ychips + yy, pl.ds(half * cc, half)]

        def sem(zz, yy, cc):
            return g_recv.at[phase, zz * ychips + yy, cc]

        def up(zz):
            return rcopy(unit(zz, y, core), unit(zz, y, core), z_send.at[phase, 0, zz], sem(zz, y, core), dev(z + 1, y, core))

        def down(zz):
            return rcopy(unit(zz, y, core), unit(zz, y, core), z_send.at[phase, 1, zz], sem(zz, y, core), dev(z - 1, y, core))

        def side(zz):
            return rcopy(unit(zz, y, core), unit(zz, y, core), y_send.at[phase, zz], sem(zz, y, core), dev(z, 1 - y, core))

        def over(zz, yy):
            return rcopy(unit(zz, yy, core), unit(zz, yy, core), c_send.at[phase, zz * ychips + yy], sem(zz, yy, core), sib)

        def arrived(zz, yy, cc):
            rcopy(unit(zz, yy, cc), unit(zz, yy, cc), c_send.at[phase, 0], sem(zz, yy, cc), sib).wait_recv()

        def onward(zz):
            if ychips > 1:
                side(zz).start()
            over(zz, y).start()

        def from_side(t):
            for zz in ([z] if t == 0 else [z - t, z + t]):
                @pl.when((zz >= 0) & (zz < zchips))
                def _():
                    arrived(zz, 1 - y, core)
                    over(zz, 1 - y).start()

        @pl.when(z + 1 < zchips)
        def _():
            up(z).start()

        @pl.when(z > 0)
        def _():
            down(z).start()

        onward(z)
        for t in range(1, zchips):
            @pl.when(z - t >= 0)
            def _():
                arrived(z - t, y, core)

                @pl.when(z + 1 < zchips)
                def _():
                    up(z - t).start()

                onward(z - t)

            @pl.when(z + t < zchips)
            def _():
                arrived(z + t, y, core)

                @pl.when(z > 0)
                def _():
                    down(z + t).start()

                onward(z + t)

            if ychips > 1:
                from_side(t - 1)
        if ychips > 1:
            from_side(zchips - 1)

        @pl.loop(0, chips)
        def _(m):
            arrived(m // ychips, lax.rem(m, ychips), 1 - core)

        def finish():
            for zz in range(zchips):
                @pl.when((z + 1 < zchips) & (zz <= z))
                def _():
                    up(zz).wait_send()

                @pl.when((z > 0) & (zz >= z))
                def _():
                    down(zz).wait_send()

                if ychips > 1:
                    side(zz).wait_send()
                for yy in range(ychips):
                    over(zz, yy).wait_send()

        return finish

    def sparse(g, tiles, index, cb):
        step = 4

        def body(i, acc):
            xs = [g[:, index[cb, step * i + u]].reshape(rows, 128) for u in range(step)]
            w = tiles[cb, pl.ds(step * i, step)].reshape(step * 128, 128)
            return acc + jnp.dot(jnp.concatenate(xs, axis=1), w, preferred_element_type=F32)

        return lax.fori_loop(0, keep // step, body, jnp.zeros((rows, 128), F32)).reshape(wide, SUB, 128)

    def a2a(phase, send, recv):
        def one(s):
            peer = lax.rem(me + s, wide)
            return rcopy(send.at[peer], recv.at[me], a_send.at[phase, peer], a_recv.at[phase, me], peer)

        def other(s):
            peer = lax.rem(me + s, wide)
            return rcopy(send.at[peer], recv.at[peer], a_send.at[phase, peer], a_recv.at[phase, peer], peer)

        @pl.loop(1, wide)
        def _(s):
            one(s).start()

        recv[me] = send[me]

        def wait():
            @pl.loop(1, wide)
            def _(s):
                other(s).wait_recv()

        def finish():
            @pl.loop(1, wide)
            def _(s):
                other(s).wait_send()

        return wait, finish

    def received(recv):
        out = []
        for d in range(wide):
            for i in range(recv.shape[1]):
                v = recv[d, i].astype(F32)
                out.extend([v[:SUB], v[SUB:]] if paired else [v])
        return out

    finishes = []
    cp1 = exchange(0, own1, sib1, g1)

    lane = lax.broadcasted_iota(jnp.int32, (SUB, 128), 1)
    sub = lax.broadcasted_iota(jnp.int32, (SUB, 128), 0)
    pos = jnp.zeros((SUB, 128), F32)
    for b in range(seqs):
        pos = jnp.where(sub == b, lengths[b].astype(F32), pos)
    turn = jnp.exp(-jnp.log(F32(10000.0)) * 2.0 * lax.rem(lane, 64).astype(F32) / 128.0)
    angle = pos * turn
    cos = jnp.cos(angle)
    sin = jnp.where(lane < 64, -jnp.sin(angle), jnp.sin(angle))

    def rope(v):
        return v * cos + pltpu.roll(v, 64, 1) * sin

    loads[0].wait()

    def build():
        for rb in range(nb):
            cols = [jnp.where(k < kv_count[rb], kv_cols[rb, k], -1) for k in range(slots)]
            for cc in range(kvb):
                at = jnp.int32(-1)
                for k in range(slots):
                    at = jnp.where(cols[k] == cc, k, at)
                tile = kt[rb, jnp.maximum(at, 0)]
                dense[128 * rb:128 * (rb + 1), 128 * cc:128 * (cc + 1)] = jnp.where(at >= 0, tile, jnp.zeros_like(tile))

    build()
    finishes.append(gather(0, g1))

    xk = jnp.concatenate([g1[:, nb * me + i].reshape(rows, 128) for i in range(nb)], axis=1)
    for i in range(kvb // 2):
        res = jnp.dot(xk, dense[:, 256 * i:256 * (i + 1)], preferred_element_type=F32)
        both = pack([res[:, :128].reshape(wide, SUB, 128), res[:, 128:].reshape(wide, SUB, 128)], True)[0]
        both = both.reshape(chips, 2, 16, 128)
        for cc in range(2):
            kp[cc, :, i] = both[:, cc]
    cpk = rcopy(kp.at[1 - core], kr, x_send.at[2], x_recv.at[2], sib)
    cpk.start()

    loads[1].wait()
    qb = [sparse(g1, qt, q_rows, cb) for cb in range(nb)]
    for i, v in enumerate(pack(qb, paired)):
        qs[:, i] = v
    q_wait, q_finish = a2a(0, qs, qr)

    cpk.wait_recv()

    @pl.loop(0, chips)
    def _(m):
        ks[m] = (kp[core, m].astype(F32) + kr[m].astype(F32)).astype(BF16)

    def kv_copy(s, at_peer):
        other = lax.rem(chip + s, chips)
        return rcopy(ks.at[other], kf.at[chip if at_peer else other], k_send.at[other],
                     k_recv.at[chip if at_peer else other], other * 2 + core)

    @pl.loop(1, chips)
    def _(s):
        kv_copy(s, True).start()

    kf[chip] = ks[chip]

    q_wait()
    for h, v in enumerate(received(qr)):
        qrot[SUB * h:SUB * (h + 1), :] = rope(v).astype(BF16).astype(F32)

    @pl.loop(1, chips)
    def _(s):
        kv_copy(s, False).wait_recv()

    for i in range(kvb // 2):
        total = kf[0, i].astype(F32)
        for m in range(1, chips):
            total = total + kf[m, i].astype(F32)
        for u in range(2):
            blk = 2 * i + u
            v = total[SUB * u:SUB * (u + 1)]
            if blk < groups:
                v = rope(v).astype(BF16)
                knew[SUB * blk:SUB * (blk + 1), :] = v.astype(F32)
            else:
                v = v.astype(BF16)
                vnew[SUB * (blk - groups):SUB * (blk - groups + 1), :] = v.astype(F32)
            new_kv[:, 128 * blk:128 * (blk + 1)] = v

    loads[2].wait()
    loads[3].wait()
    scale = 128 ** -0.5
    place = lax.broadcasted_iota(jnp.int32, (blocks, cache), 1)
    mine = lax.broadcasted_iota(jnp.int32, (blocks, groups), 0) // repeat == lax.broadcasted_iota(jnp.int32, (blocks, groups), 1)
    nt = (((1,), (1,)), ((), ()))

    @pl.loop(0, seqs)
    def _(b):
        q = qrot[pl.ds(b, blocks, stride=SUB), :]
        kn = knew[pl.ds(b, groups, stride=SUB), :]
        vn = vnew[pl.ds(b, groups, stride=SUB), :]
        s = jnp.concatenate([
            lax.dot_general(q[repeat * g:repeat * (g + 1)].astype(BF16), kc[b, g], nt, preferred_element_type=F32)
            for g in range(groups)], axis=0) * scale
        own = lax.dot_general(q.astype(BF16), kn.astype(BF16), nt, preferred_element_type=F32)
        own = jnp.sum(jnp.where(mine, own, 0.0), axis=1, keepdims=True) * scale
        s = jnp.where(place < lengths[b], s, -jnp.inf)
        top = jnp.maximum(jnp.max(s, axis=1, keepdims=True), own)
        e = jnp.exp(s - top)
        eo = jnp.exp(own - top)
        inv = 1.0 / (jnp.sum(e, axis=1, keepdims=True) + eo)
        w = e * inv
        wo = (eo * inv).astype(BF16).astype(F32)
        c = jnp.concatenate([
            jnp.dot(w[repeat * g:repeat * (g + 1)].astype(BF16), vc[b, g], preferred_element_type=F32)
            + wo[repeat * g:repeat * (g + 1)] * vn[g:g + 1]
            for g in range(groups)], axis=0)
        own2[pl.ds(b, blocks, stride=SUB), :] = c.astype(BF16).astype(F32)

    cp2 = exchange(1, own2, sib2, g2)
    finishes.append(gather(1, g2))

    loads[4].wait()
    ob = [sparse(g2, ot, o_rows, cb) for cb in range(nb)]
    for i, v in enumerate(pack(ob, paired)):
        os_[:, i] = v
    o_wait, o_finish = a2a(1, os_, or_)
    cp1.wait_send()
    cp2.wait_send()
    cpk.wait_send()
    for f in finishes:
        f()
    q_finish()

    @pl.loop(1, chips)
    def _(s):
        kv_copy(s, False).wait_send()

    o_wait()
    for h, v in enumerate(received(or_)):
        mixed[:, 128 * h:128 * (h + 1)] = v.astype(BF16)
    o_finish()


def body(wide, hidden_in, norm_gain, q_tiles, q_rows, kv_tiles, kv_cols, kv_count, o_tiles, o_rows, k_cache, v_cache, lengths):
    nb, keep, side, _ = q_tiles.shape
    seqs, groups, cache, _ = k_cache.shape
    blocks = hidden_in.shape[1] // side
    kvb = 2 * groups
    chips = wide // 2
    ychips = 2 if wide == 16 else 1
    zchips = chips // ychips
    share = (wide, nb // 2, 16, side) if nb % 2 == 0 else (wide, nb, SUB, side)
    share_type = BF16 if nb % 2 == 0 else F32
    V = pltpu.VMEM
    dma = pltpu.SemaphoreType.DMA
    smem = pl.BlockSpec(memory_space=pltpu.SMEM)
    vmem = pl.BlockSpec(memory_space=pltpu.VMEM)
    hbm = pl.BlockSpec(memory_space=pl.ANY)
    return pl.pallas_call(
        functools.partial(kernel, wide, ychips),
        out_shape=(
            jax.ShapeDtypeStruct(hidden_in.shape, BF16),
            jax.ShapeDtypeStruct((seqs, kvb * side), BF16),
        ),
        in_specs=[smem] * 5 + [vmem] * 2 + [hbm] * 5,
        out_specs=(vmem, vmem),
        scratch_shapes=[
            V(q_tiles.shape, BF16), V(kv_tiles.shape, BF16), V(o_tiles.shape, BF16),
            V(k_cache.shape, BF16), V(v_cache.shape, BF16),
            V((blocks * SUB, side), F32), V((blocks // 2 * SUB, side), F32),
            V((blocks * SUB, side), F32), V((blocks // 2 * SUB, side), F32),
            V((chips, blocks, 16, side), BF16), V((chips, blocks, 16, side), BF16),
            V((nb * side, kvb * side), BF16),
            V((2, chips, kvb // 2, 16, side), BF16), V((chips, kvb // 2, 16, side), BF16),
            V((chips, kvb // 2, 16, side), BF16), V((chips, kvb // 2, 16, side), BF16),
            V(share, share_type), V(share, share_type), V(share, share_type), V(share, share_type),
            V((blocks * SUB, side), F32), V((groups * SUB, side), F32), V((groups * SUB, side), F32),
            dma((5,)), dma((3,)), dma((3,)), dma((2, 2, zchips)), dma((2, zchips)), dma((2, chips)),
            dma((2, chips, 2)), dma((chips,)), dma((chips,)), dma((2, wide)), dma((2, wide)),
        ],
        compiler_params=pltpu.CompilerParams(
            collective_id=0, has_side_effects=True, vmem_limit_bytes=60 * 1024 * 1024),
    )(lengths, q_rows, kv_cols, kv_count, o_rows, hidden_in, norm_gain.reshape(blocks, side),
      q_tiles, kv_tiles, o_tiles, k_cache, v_cache)


def solution(mesh):
    return jax.shard_map(
        functools.partial(body, mesh.shape["wide"]),
        mesh=mesh,
        in_specs=(
            P(("group", "wide"), None),
            P(),
            P("wide", None, None, None),
            P("wide", None),
            P("wide", None, None, None),
            P("wide", None),
            P("wide"),
            P("wide", None, None, None),
            P("wide", None),
            P(("group", "wide"), None, None, None),
            P(("group", "wide"), None, None, None),
            P(("group", "wide")),
        ),
        out_specs=(P(("group", "wide"), None), P(("group", "wide"), None)),
        check_vma=False,
    )
```

time: 243 us -> 79.6 us (0.33)
  waiting for transfers between devices: 158 us -> 0 us
  Pallas kernels: 0 us -> 75.8 us
  local copies, waits for them, and re-layouts: 31.1 us -> 2.94 us
  matrix products: 18.7 us -> 0 us
  starting transfers between devices: 14.7 us -> 0 us
  between operations: 14 us -> 0.64 us
  other arithmetic: 5.94 us -> 0 us
    all_gather x2 -> x0, waiting for transfers between devices: 80.9 us -> none  [the longest x1 41.9 us: body(): lax.all_gather(normed, 'wide', axis=0, tiled=True)]
    pallas_call x0 -> x1, Pallas kernels: none -> 75.8 us  [body(): pl.pallas_call(functools.partial(kernel, wide, ychips), out_shape=(jax.Sh...]
    reduce_scatter x1 -> x0, waiting for transfers between devices: 54.1 us -> none  [body(): lax.psum_scatter(kv_terms(slices, kv_tiles, kv_cols, kv_count, kv_blocks)...]
    all_to_all x3 -> x0, waiting for transfers between devices: 21.9 us -> none  [the longest x1 7.5 us: body(): lax.all_to_all(projected, 'wide', split_axis=0, concat_axis=1, tiled=True)]
    dot_general x7 -> x0, matrix products: 18.7 us -> none  [the longest x2 9.54 us: sparse_columns(): jnp.einsum('rckd,ckde->rce', chosen, tiles, preferred_element_type=jnp.fl...]
    all_to_all x3 -> x0, starting transfers between devices: 14.4 us -> none  [the longest x1 7.39 us: body(): lax.all_to_all(normed, 'wide', split_axis=1, concat_axis=0, tiled=True)]
    gather x2 -> x0, local copies, waits for them, and re-layouts: 9.26 us -> none  [sparse_columns(): chosen = jnp.take(blocks_x, index, axis=1)]
    reshape x4 -> x0, local copies, waits for them, and re-layouts: 8.94 us -> none  [the longest x2 8.14 us: sparse_columns(): blocks_x = rows_x.reshape(count, -1, side)]
  transfers between devices with their start and end apart: 6 -> 0, of which waited for: 6 -> 0; matrix products, arithmetic and copies ran while one was open for 1% -> 0% of each run, Pallas kernels for 0% -> 0%
where the time goes in v1:
time: 79.6 us; the launch traced here: 79.4 us
  Pallas kernels  75.8 us (95%)
  local copies, waits for them, and re-layouts  2.94 us (4%)
    pallas_call x1, Pallas kernels, body(): pl.pallas_call(functools.partial(kernel, wide, ychips), out_shape=(jax.Sh...  75.8 us
    unnamed x2, local copies, waits for them, and re-layouts  2.94 us

profile of v1, /device:TPU:0, one launch (start us, length us, event | category | flops | bytes accessed | tf_op | source)
XLA Modules:
  0.0 79.4 jit_solution(3268950675779428150)
XLA Ops:
  0.6 75.8 %shard_map.131 = (bf16[8,8192]{1,0:T(8,128)(2,1)}, bf16[8,2048]{1,0:T(8,128)(2,1)}) custom-call(s32[8]{0:T(128)} %lengths.1, s32[4,32]{1,0:T(4,128)} %q_rows.1, s32[4,12]{1,0:T(4,128)} %kv_cols.1, s32[4]{0:T(128)} %kv_count.1, s32[4,32]{1,0:T(4,128)} %o_rows.1, bf16[8,8192]{1,0:T(8,128)(2,1)} %hidden.1, f32[64,128]{1,0:T(8,128)} %bitcast.1, ...), custom_call_target="tpu_custom_call" | custom-call | tf_op jit(solution)/shard_map/pallas_call | solution.py:386
  76.4 1.6 %copy.16 = bf16[8,8192]{1,0:T(8,128)(2,1)} copy(bf16[8,8192]{1,0:T(8,128)(2,1)} %get-tuple-element.4) | data formatting | bytes 262144
  78.0 1.4 %copy.17 = bf16[8,2048]{1,0:T(8,128)(2,1)} copy(bf16[8,2048]{1,0:T(8,128)(2,1)} %get-tuple-element.5) | data formatting | bytes 65536

commit v2 on v1

--- a/solution.py
+++ b/solution.py
@@ -11,6 +11,7 @@
 F32 = jnp.float32
 BF16 = jnp.bfloat16
 SUB = 8
+CUT = 2
 
 
 def pack(blocks, paired):
@@ -24,13 +25,14 @@
 
 def kernel(
     wide, ychips,
-    lengths, q_rows, kv_cols, kv_count, o_rows, hidden, gain,
+    lengths_hbm, qrows_hbm, kvcols_hbm, kvcount_hbm, orows_hbm, hidden_hbm, gain_hbm,
     q_hbm, kv_hbm, o_hbm, k_hbm, v_hbm,
     mixed, new_kv,
+    lengths, q_rows, kv_cols, kv_count, o_rows, hidden, gain,
     qt, kt, ot, kc, vc,
     own1, sib1, own2, sib2, g1, g2, dense,
-    kp, kr, ks, kf, qs, qr, os_, or_, qrot, knew, vnew,
-    load_sem, x_send, x_recv, z_send, y_send, c_send, g_recv,
+    kp, kr, ks, kf, qs, qr, os_, or_, qrot, knew, vnew, tops, totals,
+    small_sem, load_sem, x_send, x_recv, z_send, y_send, c_send, g_recv,
     k_send, k_recv, a_send, a_recv,
 ):
     chips = wide // 2
@@ -65,11 +67,18 @@
     def _(s):
         pl.semaphore_signal(barrier, inc=1, device_id={"wide": lax.rem(me + s, wide)}, device_id_type=MESH)
 
+    smalls = [pltpu.make_async_copy(a, b, small_sem.at[i])
+              for i, (a, b) in enumerate(((hidden_hbm, hidden), (gain_hbm, gain), (kvcount_hbm, kv_count), (kvcols_hbm, kv_cols),
+                                          (qrows_hbm, q_rows), (lengths_hbm, lengths), (orows_hbm, o_rows)))]
+    for cp in smalls:
+        cp.start()
     loads = [pltpu.make_async_copy(a, b, load_sem.at[i])
              for i, (a, b) in enumerate(((kv_hbm, kt), (q_hbm, qt), (k_hbm, kc), (v_hbm, vc), (o_hbm, ot)))]
     for cp in loads:
         cp.start()
 
+    for cp in smalls:
+        cp.wait()
     x = hidden[...].astype(F32)
     r = lax.rsqrt(jnp.mean(x * x, axis=1, keepdims=True) + 1e-05)
     for j in range(blocks):
@@ -92,92 +101,99 @@
         return cp
 
     def gather(phase, g):
-        def unit(zz, yy, cc):
-            return g.at[zz * ychips + yy, pl.ds(half * cc, half)]
-
-        def sem(zz, yy, cc):
-            return g_recv.at[phase, zz * ychips + yy, cc]
-
-        def up(zz):
-            return rcopy(unit(zz, y, core), unit(zz, y, core), z_send.at[phase, 0, zz], sem(zz, y, core), dev(z + 1, y, core))
-
-        def down(zz):
-            return rcopy(unit(zz, y, core), unit(zz, y, core), z_send.at[phase, 1, zz], sem(zz, y, core), dev(z - 1, y, core))
-
-        def side(zz):
-            return rcopy(unit(zz, y, core), unit(zz, y, core), y_send.at[phase, zz], sem(zz, y, core), dev(z, 1 - y, core))
-
-        def over(zz, yy):
-            return rcopy(unit(zz, yy, core), unit(zz, yy, core), c_send.at[phase, zz * ychips + yy], sem(zz, yy, core), sib)
-
-        def arrived(zz, yy, cc):
-            rcopy(unit(zz, yy, cc), unit(zz, yy, cc), c_send.at[phase, 0], sem(zz, yy, cc), sib).wait_recv()
-
-        def onward(zz):
+        span = half // CUT
+
+        def unit(zz, yy, cc, h):
+            return g.at[zz * ychips + yy, pl.ds(half * cc + span * h, span)]
+
+        def sem(zz, yy, cc, h):
+            return g_recv.at[phase, zz * ychips + yy, cc, h]
+
+        def up(zz, h):
+            return rcopy(unit(zz, y, core, h), unit(zz, y, core, h), z_send.at[phase, 0, zz, h], sem(zz, y, core, h), dev(z + 1, y, core))
+
+        def down(zz, h):
+            return rcopy(unit(zz, y, core, h), unit(zz, y, core, h), z_send.at[phase, 1, zz, h], sem(zz, y, core, h), dev(z - 1, y, core))
+
+        def side(zz, h):
+            return rcopy(unit(zz, y, core, h), unit(zz, y, core, h), y_send.at[phase, zz, h], sem(zz, y, core, h), dev(z, 1 - y, core))
+
+        def over(zz, yy, h):
+            return rcopy(unit(zz, yy, core, h), unit(zz, yy, core, h), c_send.at[phase, zz * ychips + yy, h], sem(zz, yy, core, h), sib)
+
+        def arrived(zz, yy, cc, h):
+            rcopy(unit(zz, yy, cc, h), unit(zz, yy, cc, h), c_send.at[phase, 0, h], sem(zz, yy, cc, h), sib).wait_recv()
+
+        def onward(zz, h):
             if ychips > 1:
-                side(zz).start()
-            over(zz, y).start()
-
-        def from_side(t):
+                side(zz, h).start()
+            over(zz, y, h).start()
+
+        def from_side(t, h):
             for zz in ([z] if t == 0 else [z - t, z + t]):
                 @pl.when((zz >= 0) & (zz < zchips))
                 def _():
-                    arrived(zz, 1 - y, core)
-                    over(zz, 1 - y).start()
-
-        @pl.when(z + 1 < zchips)
-        def _():
-            up(z).start()
-
-        @pl.when(z > 0)
-        def _():
-            down(z).start()
-
-        onward(z)
+                    arrived(zz, 1 - y, core, h)
+                    over(zz, 1 - y, h).start()
+
+        for h in range(CUT):
+            @pl.when(z + 1 < zchips)
+            def _():
+                up(z, h).start()
+
+            @pl.when(z > 0)
+            def _():
+                down(z, h).start()
+
+            onward(z, h)
         for t in range(1, zchips):
-            @pl.when(z - t >= 0)
-            def _():
-                arrived(z - t, y, core)
-
-                @pl.when(z + 1 < zchips)
+            for h in range(CUT):
+                @pl.when(z - t >= 0)
                 def _():
-                    up(z - t).start()
-
-                onward(z - t)
-
-            @pl.when(z + t < zchips)
-            def _():
-                arrived(z + t, y, core)
-
-                @pl.when(z > 0)
+                    arrived(z - t, y, core, h)
+
+                    @pl.when(z + 1 < zchips)
+                    def _():
+                        up(z - t, h).start()
+
+                    onward(z - t, h)
+
+                @pl.when(z + t < zchips)
                 def _():
-                    down(z + t).start()
-
-                onward(z + t)
-
-            if ychips > 1:
-                from_side(t - 1)
+                    arrived(z + t, y, core, h)
+
+                    @pl.when(z > 0)
+                    def _():
+                        down(z + t, h).start()
+
+                    onward(z + t, h)
+
+                if ychips > 1:
+                    from_side(t - 1, h)
         if ychips > 1:
-            from_side(zchips - 1)
+            for h in range(CUT):
+                from_side(zchips - 1, h)
 
         @pl.loop(0, chips)
         def _(m):
-            arrived(m // ychips, lax.rem(m, ychips), 1 - core)
+            for h in range(CUT):
+                arrived(m // ychips, lax.rem(m, ychips), 1 - core, h)
 
         def finish():
             for zz in range(zchips):
-                @pl.when((z + 1 < zchips) & (zz <= z))
-                def _():
-                    up(zz).wait_send()
-
-                @pl.when((z > 0) & (zz >= z))
-                def _():
-                    down(zz).wait_send()
-
-                if ychips > 1:
-                    side(zz).wait_send()
-                for yy in range(ychips):
-                    over(zz, yy).wait_send()
+                for h in range(CUT):
+                    @pl.when((z + 1 < zchips) & (zz <= z))
+                    def _():
+                        up(zz, h).wait_send()
+
+                    @pl.when((z > 0) & (zz >= z))
+                    def _():
+                        down(zz, h).wait_send()
+
+                    if ychips > 1:
+                        side(zz, h).wait_send()
+                    for yy in range(ychips):
+                        over(zz, yy, h).wait_send()
 
         return finish
 
@@ -189,40 +205,43 @@
             w = tiles[cb, pl.ds(step * i, step)].reshape(step * 128, 128)
             return acc + jnp.dot(jnp.concatenate(xs, axis=1), w, preferred_element_type=F32)
 
-        return lax.fori_loop(0, keep // step, body, jnp.zeros((rows, 128), F32)).reshape(wide, SUB, 128)
+        return lax.fori_loop(0, keep // step, body, jnp.zeros((rows, 128), F32), unroll=True).reshape(wide, SUB, 128)
 
     def a2a(phase, send, recv):
-        def one(s):
-            peer = lax.rem(me + s, wide)
-            return rcopy(send.at[peer], recv.at[me], a_send.at[phase, peer], a_recv.at[phase, me], peer)
-
-        def other(s):
-            peer = lax.rem(me + s, wide)
-            return rcopy(send.at[peer], recv.at[peer], a_send.at[phase, peer], a_recv.at[phase, peer], peer)
-
-        @pl.loop(1, wide)
-        def _(s):
-            one(s).start()
-
-        recv[me] = send[me]
-
-        def wait():
+        parts = send.shape[0]
+
+        def copy(i, peer, slot):
+            return rcopy(send.at[i, peer], recv.at[i, slot], a_send.at[phase, i, peer], a_recv.at[phase, i, slot], peer)
+
+        def start(i):
             @pl.loop(1, wide)
             def _(s):
-                other(s).wait_recv()
+                off = jnp.where(s <= chips, s + chips - 1, s - chips)
+                copy(i, lax.rem(me + off, wide), me).start()
+
+            recv[i, me] = send[i, me]
+
+        def wait():
+            for i in range(parts):
+                @pl.loop(1, wide)
+                def _(s):
+                    peer = lax.rem(me + s, wide)
+                    copy(i, peer, peer).wait_recv()
 
         def finish():
-            @pl.loop(1, wide)
-            def _(s):
-                other(s).wait_send()
-
-        return wait, finish
+            for i in range(parts):
+                @pl.loop(1, wide)
+                def _(s):
+                    peer = lax.rem(me + s, wide)
+                    copy(i, peer, peer).wait_send()
+
+        return start, wait, finish
 
     def received(recv):
         out = []
         for d in range(wide):
-            for i in range(recv.shape[1]):
-                v = recv[d, i].astype(F32)
+            for i in range(recv.shape[0]):
+                v = recv[i, d].astype(F32)
                 out.extend([v[:SUB], v[SUB:]] if paired else [v])
         return out
 
@@ -268,10 +287,11 @@
     cpk.start()
 
     loads[1].wait()
-    qb = [sparse(g1, qt, q_rows, cb) for cb in range(nb)]
-    for i, v in enumerate(pack(qb, paired)):
-        qs[:, i] = v
-    q_wait, q_finish = a2a(0, qs, qr)
+    q_start, q_wait, q_finish = a2a(0, qs, qr)
+    per = 2 if paired else 1
+    for i in range(nb // per):
+        qs[i] = pack([sparse(g1, qt, q_rows, per * i + u) for u in range(per)], paired)[0]
+        q_start(i)
 
     cpk.wait_recv()
 
@@ -293,6 +313,27 @@
     q_wait()
     for h, v in enumerate(received(qr)):
         qrot[SUB * h:SUB * (h + 1), :] = rope(v).astype(BF16).astype(F32)
+
+    loads[2].wait()
+    loads[3].wait()
+    scale = 128 ** -0.5
+    place = lax.broadcasted_iota(jnp.int32, (blocks, cache), 1)
+    nt = (((1,), (1,)), ((), ()))
+
+    @pl.loop(0, seqs)
+    def _(b):
+        q = qrot[pl.ds(b, blocks, stride=SUB), :]
+        s = jnp.concatenate([
+            lax.dot_general(q[repeat * g:repeat * (g + 1)].astype(BF16), kc[b, g], nt, preferred_element_type=F32)
+            for g in range(groups)], axis=0) * scale
+        s = jnp.where(place < lengths[b], s, -jnp.inf)
+        top = jnp.max(s, axis=1, keepdims=True)
+        e = jnp.exp(s - top)
+        tops[pl.ds(b, blocks, stride=SUB), :] = jnp.broadcast_to(top, (blocks, 128))
+        totals[pl.ds(b, blocks, stride=SUB), :] = jnp.broadcast_to(jnp.sum(e, axis=1, keepdims=True), (blocks, 128))
+        own2[pl.ds(b, blocks, stride=SUB), :] = jnp.concatenate([
+            jnp.dot(e[repeat * g:repeat * (g + 1)].astype(BF16), vc[b, g], preferred_element_type=F32)
+            for g in range(groups)], axis=0)
 
     @pl.loop(1, chips)
     def _(s):
@@ -313,44 +354,25 @@
                 vnew[SUB * (blk - groups):SUB * (blk - groups + 1), :] = v.astype(F32)
             new_kv[:, 128 * blk:128 * (blk + 1)] = v
 
-    loads[2].wait()
-    loads[3].wait()
-    scale = 128 ** -0.5
-    place = lax.broadcasted_iota(jnp.int32, (blocks, cache), 1)
-    mine = lax.broadcasted_iota(jnp.int32, (blocks, groups), 0) // repeat == lax.broadcasted_iota(jnp.int32, (blocks, groups), 1)
-    nt = (((1,), (1,)), ((), ()))
-
-    @pl.loop(0, seqs)
-    def _(b):
-        q = qrot[pl.ds(b, blocks, stride=SUB), :]
-        kn = knew[pl.ds(b, groups, stride=SUB), :]
-        vn = vnew[pl.ds(b, groups, stride=SUB), :]
-        s = jnp.concatenate([
-            lax.dot_general(q[repeat * g:repeat * (g + 1)].astype(BF16), kc[b, g], nt, preferred_element_type=F32)
-            for g in range(groups)], axis=0) * scale
-        own = lax.dot_general(q.astype(BF16), kn.astype(BF16), nt, preferred_element_type=F32)
-        own = jnp.sum(jnp.where(mine, own, 0.0), axis=1, keepdims=True) * scale
-        s = jnp.where(place < lengths[b], s, -jnp.inf)
-        top = jnp.maximum(jnp.max(s, axis=1, keepdims=True), own)
-        e = jnp.exp(s - top)
-        eo = jnp.exp(own - top)
-        inv = 1.0 / (jnp.sum(e, axis=1, keepdims=True) + eo)
-        w = e * inv
-        wo = (eo * inv).astype(BF16).astype(F32)
-        c = jnp.concatenate([
-            jnp.dot(w[repeat * g:repeat * (g + 1)].astype(BF16), vc[b, g], preferred_element_type=F32)
-            + wo[repeat * g:repeat * (g + 1)] * vn[g:g + 1]
-            for g in range(groups)], axis=0)
-        own2[pl.ds(b, blocks, stride=SUB), :] = c.astype(BF16).astype(F32)
+    for h in range(blocks):
+        at = slice(SUB * h, SUB * (h + 1))
+        grp = slice(SUB * (h // repeat), SUB * (h // repeat + 1))
+        own = jnp.sum(qrot[at, :] * knew[grp, :], axis=1, keepdims=True) * scale
+        top = tops[at, :]
+        both = jnp.maximum(top, own)
+        old = jnp.exp(top - both)
+        new = jnp.exp(own - both)
+        c = (own2[at, :] * old + new * vnew[grp, :]) / (totals[at, :] * old + new)
+        own2[at, :] = c.astype(BF16).astype(F32)
 
     cp2 = exchange(1, own2, sib2, g2)
     finishes.append(gather(1, g2))
 
     loads[4].wait()
-    ob = [sparse(g2, ot, o_rows, cb) for cb in range(nb)]
-    for i, v in enumerate(pack(ob, paired)):
-        os_[:, i] = v
-    o_wait, o_finish = a2a(1, os_, or_)
+    o_start, o_wait, o_finish = a2a(1, os_, or_)
+    for i in range(nb // per):
+        os_[i] = pack([sparse(g2, ot, o_rows, per * i + u) for u in range(per)], paired)[0]
+        o_start(i)
     cp1.wait_send()
     cp2.wait_send()
     cpk.wait_send()
@@ -376,11 +398,11 @@
     chips = wide // 2
     ychips = 2 if wide == 16 else 1
     zchips = chips // ychips
-    share = (wide, nb // 2, 16, side) if nb % 2 == 0 else (wide, nb, SUB, side)
+    share = (nb // 2, wide, 16, side) if nb % 2 == 0 else (nb, wide, SUB, side)
     share_type = BF16 if nb % 2 == 0 else F32
     V = pltpu.VMEM
     dma = pltpu.SemaphoreType.DMA
-    smem = pl.BlockSpec(memory_space=pltpu.SMEM)
+    S = pltpu.SMEM
     vmem = pl.BlockSpec(memory_space=pltpu.VMEM)
     hbm = pl.BlockSpec(memory_space=pl.ANY)
     return pl.pallas_call(
@@ -389,9 +411,12 @@
             jax.ShapeDtypeStruct(hidden_in.shape, BF16),
             jax.ShapeDtypeStruct((seqs, kvb * side), BF16),
         ),
-        in_specs=[smem] * 5 + [vmem] * 2 + [hbm] * 5,
+        in_specs=[hbm] * 12,
         out_specs=(vmem, vmem),
         scratch_shapes=[
+            S(lengths.shape, jnp.int32), S(q_rows.shape, jnp.int32), S(kv_cols.shape, jnp.int32),
+            S(kv_count.shape, jnp.int32), S(o_rows.shape, jnp.int32),
+            V(hidden_in.shape, BF16), V((blocks, side), F32),
             V(q_tiles.shape, BF16), V(kv_tiles.shape, BF16), V(o_tiles.shape, BF16),
             V(k_cache.shape, BF16), V(v_cache.shape, BF16),
             V((blocks * SUB, side), F32), V((blocks // 2 * SUB, side), F32),
@@ -402,8 +427,9 @@
             V((chips, kvb // 2, 16, side), BF16), V((chips, kvb // 2, 16, side), BF16),
             V(share, share_type), V(share, share_type), V(share, share_type), V(share, share_type),
             V((blocks * SUB, side), F32), V((groups * SUB, side), F32), V((groups * SUB, side), F32),
-            dma((5,)), dma((3,)), dma((3,)), dma((2, 2, zchips)), dma((2, zchips)), dma((2, chips)),
-            dma((2, chips, 2)), dma((chips,)), dma((chips,)), dma((2, wide)), dma((2, wide)),
+            V((blocks * SUB, side), F32), V((blocks * SUB, side), F32),
+            dma((7,)), dma((5,)), dma((3,)), dma((3,)), dma((2, 2, zchips, CUT)), dma((2, zchips, CUT)), dma((2, chips, CUT)),
+            dma((2, chips, 2, CUT)), dma((chips,)), dma((chips,)), dma((2, share[0], wide)), dma((2, share[0], wide)),
         ],
         compiler_params=pltpu.CompilerParams(
             collective_id=0, has_side_effects=True, vmem_limit_bytes=60 * 1024 * 1024),

time: 79.6 us -> 65.6 us (0.82)
  Pallas kernels: 75.8 us -> 61.8 us
    pallas_call x1, Pallas kernels: 75.8 us -> 61.8 us  [body(): pl.pallas_call(functools.partial(kernel, wide, ychips), out_shape=(jax.Sh...]
where the time goes in v2:
time: 65.6 us; the launch traced here: 65.3 us
  Pallas kernels  61.8 us (94%)
  local copies, waits for them, and re-layouts  2.94 us (4%)
    pallas_call x1, Pallas kernels, body(): pl.pallas_call(functools.partial(kernel, wide, ychips), out_shape=(jax.Sh...  61.8 us
    unnamed x2, local copies, waits for them, and re-layouts  2.94 us

profile of v2, /device:TPU:0, one launch (start us, length us, event | category | flops | bytes accessed | tf_op | source)
XLA Modules:
  0.0 65.3 jit_solution(2734361069453510009)
XLA Ops:
  0.6 61.8 %shard_map.131 = (bf16[8,8192]{1,0:T(8,128)(2,1)}, bf16[8,2048]{1,0:T(8,128)(2,1)}) custom-call(s32[8]{0:T(128)} %lengths_hbm.1, s32[4,32]{1,0:T(4,128)} %qrows_hbm.1, s32[4,12]{1,0:T(4,128)} %kvcols_hbm.1, s32[4]{0:T(128)} %kvcount_hbm.1, s32[4,32]{1,0:T(4,128)} %orows_hbm.1, bf16[8,8192]{1,0:T(8,128)(2,1)} %hidden_hbm.1, f32[64,128]{1,0:T(8,128)} %bitcast.1, ...), custom_call_target="tpu_custom_call" | custom-call | tf_op jit(solution)/shard_map/pallas_call | solution.py:408
  62.4 1.6 %copy.16 = bf16[8,8192]{1,0:T(8,128)(2,1)} copy(bf16[8,8192]{1,0:T(8,128)(2,1)} %get-tuple-element.4) | data formatting | bytes 262144
  64.0 1.4 %copy.17 = bf16[8,2048]{1,0:T(8,128)(2,1)} copy(bf16[8,2048]{1,0:T(8,128)(2,1)} %get-tuple-element.5) | data formatting | bytes 65536

commit v3 on v2

--- a/solution.py
+++ b/solution.py
@@ -31,7 +31,7 @@
     lengths, q_rows, kv_cols, kv_count, o_rows, hidden, gain,
     qt, kt, ot, kc, vc,
     own1, sib1, own2, sib2, g1, g2, dense,
-    kp, kr, ks, kf, qs, qr, os_, or_, qrot, knew, vnew, tops, totals,
+    kp, kr, ks, kf, qs, qr, os_, or_, qrot, knew, vnew, tops, totals, turns,
     small_sem, load_sem, x_send, x_recv, z_send, y_send, c_send, g_recv,
     k_send, k_recv, a_send, a_recv,
 ):
@@ -100,7 +100,7 @@
         g[chip, pl.ds(half * core, half)] = jnp.concatenate([first, second], axis=1).astype(BF16)
         return cp
 
-    def gather(phase, g):
+    def gather(phase, g, meanwhile=None):
         span = half // CUT
 
         def unit(zz, yy, cc, h):
@@ -146,6 +146,8 @@
                 down(z, h).start()
 
             onward(z, h)
+        if meanwhile is not None:
+            meanwhile()
         for t in range(1, zchips):
             for h in range(CUT):
                 @pl.when(z - t >= 0)
@@ -248,22 +250,20 @@
     finishes = []
     cp1 = exchange(0, own1, sib1, g1)
 
-    lane = lax.broadcasted_iota(jnp.int32, (SUB, 128), 1)
-    sub = lax.broadcasted_iota(jnp.int32, (SUB, 128), 0)
-    pos = jnp.zeros((SUB, 128), F32)
-    for b in range(seqs):
-        pos = jnp.where(sub == b, lengths[b].astype(F32), pos)
-    turn = jnp.exp(-jnp.log(F32(10000.0)) * 2.0 * lax.rem(lane, 64).astype(F32) / 128.0)
-    angle = pos * turn
-    cos = jnp.cos(angle)
-    sin = jnp.where(lane < 64, -jnp.sin(angle), jnp.sin(angle))
-
     def rope(v):
-        return v * cos + pltpu.roll(v, 64, 1) * sin
-
-    loads[0].wait()
+        return v * turns[0] + pltpu.roll(v, 64, 1) * turns[1]
 
     def build():
+        lane = lax.broadcasted_iota(jnp.int32, (SUB, 128), 1)
+        sub = lax.broadcasted_iota(jnp.int32, (SUB, 128), 0)
+        pos = jnp.zeros((SUB, 128), F32)
+        for b in range(seqs):
+            pos = jnp.where(sub == b, lengths[b].astype(F32), pos)
+        turn = jnp.exp(-jnp.log(F32(10000.0)) * 2.0 * lax.rem(lane, 64).astype(F32) / 128.0)
+        angle = pos * turn
+        turns[0] = jnp.cos(angle)
+        turns[1] = jnp.where(lane < 64, -jnp.sin(angle), jnp.sin(angle))
+        loads[0].wait()
         for rb in range(nb):
             cols = [jnp.where(k < kv_count[rb], kv_cols[rb, k], -1) for k in range(slots)]
             for cc in range(kvb):
@@ -273,8 +273,14 @@
                 tile = kt[rb, jnp.maximum(at, 0)]
                 dense[128 * rb:128 * (rb + 1), 128 * cc:128 * (cc + 1)] = jnp.where(at >= 0, tile, jnp.zeros_like(tile))
 
-    build()
-    finishes.append(gather(0, g1))
+    finishes.append(gather(0, g1, build))
+
+    loads[1].wait()
+    q_start, q_wait, q_finish = a2a(0, qs, qr)
+    per = 2 if paired else 1
+    for i in range(nb // per):
+        qs[i] = pack([sparse(g1, qt, q_rows, per * i + u) for u in range(per)], paired)[0]
+        q_start(i)
 
     xk = jnp.concatenate([g1[:, nb * me + i].reshape(rows, 128) for i in range(nb)], axis=1)
     for i in range(kvb // 2):
@@ -286,13 +292,6 @@
     cpk = rcopy(kp.at[1 - core], kr, x_send.at[2], x_recv.at[2], sib)
     cpk.start()
 
-    loads[1].wait()
-    q_start, q_wait, q_finish = a2a(0, qs, qr)
-    per = 2 if paired else 1
-    for i in range(nb // per):
-        qs[i] = pack([sparse(g1, qt, q_rows, per * i + u) for u in range(per)], paired)[0]
-        q_start(i)
-
     cpk.wait_recv()
 
     @pl.loop(0, chips)
@@ -320,7 +319,7 @@
     place = lax.broadcasted_iota(jnp.int32, (blocks, cache), 1)
     nt = (((1,), (1,)), ((), ()))
 
-    @pl.loop(0, seqs)
+    @pl.loop(0, seqs, unroll=2)
     def _(b):
         q = qrot[pl.ds(b, blocks, stride=SUB), :]
         s = jnp.concatenate([
@@ -427,7 +426,7 @@
             V((chips, kvb // 2, 16, side), BF16), V((chips, kvb // 2, 16, side), BF16),
             V(share, share_type), V(share, share_type), V(share, share_type), V(share, share_type),
             V((blocks * SUB, side), F32), V((groups * SUB, side), F32), V((groups * SUB, side), F32),
-            V((blocks * SUB, side), F32), V((blocks * SUB, side), F32),
+            V((blocks * SUB, side), F32), V((blocks * SUB, side), F32), V((2, SUB, side), F32),
             dma((7,)), dma((5,)), dma((3,)), dma((3,)), dma((2, 2, zchips, CUT)), dma((2, zchips, CUT)), dma((2, chips, CUT)),
             dma((2, chips, 2, CUT)), dma((chips,)), dma((chips,)), dma((2, share[0], wide)), dma((2, share[0], wide)),
         ],

time: 65.6 us -> 63.9 us (0.974)
  Pallas kernels: 61.8 us -> 60.1 us
    pallas_call x1, Pallas kernels: 61.8 us -> 60.1 us  [body(): pl.pallas_call(functools.partial(kernel, wide, ychips), out_shape=(jax.Sh...]
where the time goes in v3:
time: 63.9 us; the launch traced here: 63.7 us
  Pallas kernels  60.1 us (94%)
  local copies, waits for them, and re-layouts  2.94 us (5%)
  between operations  0.64 us (1%)
    pallas_call x1, Pallas kernels, body(): pl.pallas_call(functools.partial(kernel, wide, ychips), out_shape=(jax.Sh...  60.1 us
    unnamed x2, local copies, waits for them, and re-layouts  2.94 us

profile of v3, /device:TPU:0, one launch (start us, length us, event | category | flops | bytes accessed | tf_op | source)
XLA Modules:
  0.0 63.7 jit_solution(12199865805334618101)
XLA Ops:
  0.6 60.1 %shard_map.131 = (bf16[8,8192]{1,0:T(8,128)(2,1)}, bf16[8,2048]{1,0:T(8,128)(2,1)}) custom-call(s32[8]{0:T(128)} %lengths_hbm.1, s32[4,32]{1,0:T(4,128)} %qrows_hbm.1, s32[4,12]{1,0:T(4,128)} %kvcols_hbm.1, s32[4]{0:T(128)} %kvcount_hbm.1, s32[4,32]{1,0:T(4,128)} %orows_hbm.1, bf16[8,8192]{1,0:T(8,128)(2,1)} %hidden_hbm.1, f32[64,128]{1,0:T(8,128)} %bitcast.1, ...), custom_call_target="tpu_custom_call" | custom-call | tf_op jit(solution)/shard_map/pallas_call | solution.py:407
  60.8 1.6 %copy.16 = bf16[8,8192]{1,0:T(8,128)(2,1)} copy(bf16[8,8192]{1,0:T(8,128)(2,1)} %get-tuple-element.4) | data formatting | bytes 262144
  62.3 1.4 %copy.17 = bf16[8,2048]{1,0:T(8,128)(2,1)} copy(bf16[8,2048]{1,0:T(8,128)(2,1)} %get-tuple-element.5) | data formatting | bytes 65536
